TPU v7x, 32 devices: a whole 2x2x4 slice. The times are simulated.
32 devices in a mesh: groups: 2 (over y), stream: 4 (over z), tensor: 2 (over x), sub: 2 (over core).
Axes of the slice: x: 2, y: 2, z: 4, core: 2. Of those that a mesh axis runs over, the one named last changes fastest.
Arguments:
- lm_query: bfloat16 [192, 3584], P(('groups', 'stream', 'sub'), 'tensor'), parts along dimension 0, may hold values from -6 to 6
- lm_cache: bfloat16 [192, 64, 2, 512], P(('groups', 'stream', 'sub'), None, None, 'tensor'), parts along dimension 0, may hold values from -6 to 6
- language_new_pair: bfloat16 [192, 2, 512], P(('groups', 'stream', 'sub'), None, 'tensor'), parts along dimension 0, may hold values from -6 to 6
- lm_lengths: int32 [192], P('groups'), parts along dimension 0, may hold values from 21 to 64, as said below
- lm_resid: bfloat16 [192, 3584], P(('groups', 'stream'), 'sub'), parts along dimension 0, may hold values from -18 to 18
- lm_wo: bfloat16 [3584, 3584], P('tensor', 'sub'), may hold values from -0.09375 to 0.09375
- lm_gain: bfloat16 [3584], P('sub'), may hold values from 0.5 to 1.5
- lm_adapt: bfloat16 [3584, 1024], P('sub', 'tensor'), may hold values from -0.09375 to 0.09375
- det_noise: bfloat16 [192, 30, 1024], P(('groups', 'stream'), None, ('tensor', 'sub')), parts along dimension 0, may hold values from -18 to 18
- det_pending: bfloat16 [192, 29, 1024], P(('groups', 'stream'), None, ('tensor', 'sub')), parts along dimension 0, may hold values from -6 to 6
- det_cache: bfloat16 [8, 24, 60, 2, 1024], P(('groups', 'stream'), None, None, None, ('tensor', 'sub')), parts along dimension 0, may hold values from -6 to 6
- det_qkv: bfloat16 [3, 1024, 1024], P(None, None, ('tensor', 'sub')), may hold values from -0.1875 to 0.1875
- det_out: bfloat16 [1024, 1024], P(('tensor', 'sub')), may hold values from -0.1875 to 0.1875
- det_gain: bfloat16 [1024], replicated, may hold values from 0.5 to 1.5
- complete: int32 [192], P('groups'), parts along dimension 0, may hold values from 0 to 1, as said below
- owner: int32 [192], P('groups'), parts along dimension 0, may hold values from 0 to 3, as said below
- prev_owner: int32 [192], P('groups'), parts along dimension 0, may hold values from 0 to 3, as said below
Outputs:
- lm_hidden: bfloat16 [192, 3584], P(('groups', 'stream'), 'sub'), parts along dimension 0
- new_state: bfloat16 [8, 4, 6, 30, 1024], P(('groups', 'stream'), None, None, None, ('tensor', 'sub')), parts along dimension 0
There are 2 independent parts, one for each index of `groups`. A program takes and returns all parts, laid end to end along the dimension named above; an argument that names none is the same for every part. Nothing has to cross between parts.
Inputs may be any that keep to these rules, and one draw needn't show every extreme that they name: `lm_lengths`: some stream has exactly 64 valid positions. From one stream shard (streams j * 24 to (j + 1) * 24 - 1) at most 6 complete streams have the same owner, and some owner receives exactly 6 from every shard. `owner`: only the owners of complete streams matter. `prev_owner`: every owner holds exactly 24 streams' caches; at most 6 complete streams share one pair of previous and new owner, and for some new owner that many come from every previous owner.
All inputs are finite; a program needn't handle non-finite values.
Results may differ from a plain program's by a relative error of at most 0.006.
Values may be sent and summed in bfloat16 or wider, within the bound.
A program may use at most 128 MiB of HBM per device.

v0:
```python
import functools

import jax
import jax.numpy as jnp
from jax import lax
from jax.experimental import pallas as pl
from jax.experimental.pallas import tpu as pltpu
from jax.sharding import PartitionSpec as P

QUERY_HEADS = 28
KEY_VALUE_HEADS = 4
HEAD_WIDTH = 128
DHD = 64
SLOTS = 6
MESH = pl.DeviceIdType.MESH

step_size = 0.5
epsilon = 1e-06
NEG = -1e30
F32 = jnp.float32
BF16 = jnp.bfloat16


def up(n, m):
    return (n + m - 1) // m * m


def dot_nt(a, b):
    return lax.dot_general(a, b, (((1,), (1,)), ((), ())), preferred_element_type=F32)


def kernel(
    sizes,
    past_len,
    pack_ref, cpack_ref, crow_ref, order_ref, orow_ref, outidx_ref, live_ref,
    state_ref, dcache_ref, q_ref, lmx_ref, newk_ref, newv_ref, bias_ref, resid_ref, gain_ref,
    dgain_ref,
    wo_hbm, adapt_hbm, qkv_hbm, dout_hbm,
    hid_ref, out_ref,
    wo, adapt, qkv, dout,
    stsend, strecv, csend, crecv, att_all, parts, condx, condf, condpack, condsend, condrecv,
    condrf, gath, n29, lg, lgf, a_s, qb, kb, vb, mx, own, osend, orecv, res,
    w_sem, st_s, st_r, ca_s, ca_r, co_s, co_r, at_s, at_r, pa_s, pa_r, cx_s, cx_r,
    g_s, g_r, l_s, l_r, o_s, o_r,
):
    S, T, U = sizes
    NP = T * U
    me = lax.axis_index("stream")
    t_me = lax.axis_index("tensor")
    u_me = lax.axis_index("sub")
    p_me = t_me * U + u_me
    CW = state_ref.shape[2]
    TOK = state_ref.shape[1]
    SL = S * SLOTS
    KV, NS = q_ref.shape[0], q_ref.shape[1]
    NR = att_all.shape[1]
    R = QUERY_HEADS // KEY_VALUE_HEADS
    last = out_ref.shape[1] - 1

    def at_stream(d):
        return {"stream": lax.rem(me + d, S)}

    def at_part(d):
        peer = lax.rem(p_me + d, NP)
        return {"tensor": lax.div(peer, U), "sub": lax.rem(peer, U)}

    def send(src, dst, ss, rs, dev):
        c = pltpu.make_async_remote_copy(
            src_ref=src, dst_ref=dst, send_sem=ss, recv_sem=rs, device_id=dev,
            device_id_type=MESH,
        )
        c.start()
        return c

    loads = []
    for i, (s, d) in enumerate(((wo_hbm, wo), (adapt_hbm, adapt), (qkv_hbm, qkv), (dout_hbm, dout))):
        c = pltpu.make_async_copy(s, d, w_sem.at[i])
        c.start()
        loads.append(c)

    barrier = pltpu.get_barrier_semaphore()
    for d in range(1, S):
        pl.semaphore_signal(barrier, inc=1, device_id=at_stream(d), device_id_type=MESH)
    for d in range(1, NP):
        pl.semaphore_signal(barrier, inc=1, device_id=at_part(d), device_id_type=MESH)

    def pack_state(i, _):
        stsend[i] = state_ref[pack_ref[i]]
        return 0

    lax.fori_loop(0, SL, pack_state, 0)
    pl.semaphore_wait(barrier, S - 1 + NP - 1)
    st_copies = []
    for d in range(1, S):
        o = lax.rem(me + d, S)
        st_copies.append(
            send(stsend.at[pl.ds(o * SLOTS, SLOTS)], strecv.at[pl.ds(me * SLOTS, SLOTS)],
                 st_s.at[d], st_r.at[d], at_stream(d))
        )

    def pack_cache(i, _):
        csend[i] = dcache_ref[cpack_ref[i]]
        return 0

    lax.fori_loop(0, SL, pack_cache, 0)
    ca_copies = [None]
    for d in range(1, S):
        o = lax.rem(me + d, S)
        ca_copies.append(
            send(csend.at[pl.ds(o * SLOTS, SLOTS)], crecv.at[pl.ds(me * SLOTS, SLOTS)],
                 ca_s.at[d], ca_r.at[d], at_stream(d))
        )

    def keep_own(i, _):
        c = me * SLOTS + i
        strecv[c] = stsend[c]
        crecv[c] = csend[c]
        return 0

    lax.fori_loop(0, SLOTS, keep_own, 0)

    scale = HEAD_WIDTH ** (-0.5)
    bias = bias_ref[...]
    if NR > NS:
        att_all[u_me] = jnp.zeros(att_all.shape[1:], BF16)
    for kv in range(KV):
        q = q_ref[kv]
        x = lmx_ref[:, :, kv * HEAD_WIDTH:(kv + 1) * HEAD_WIDTH]
        s = lax.dot_general(q, x, (((2,), (2,)), ((0,), (0,))), preferred_element_type=F32)
        s = s * scale + bias
        s_new = jnp.sum(q.astype(F32) * newk_ref[kv], axis=-1, keepdims=True) * scale
        top = jnp.maximum(jnp.max(s, axis=-1, keepdims=True), s_new)
        w = jnp.exp(s - top)
        w_new = jnp.exp(s_new - top)
        total = jnp.sum(w, axis=-1, keepdims=True) + w_new
        w_rows = w.reshape(NS * 8, w.shape[2])
        w_odd = pltpu.roll(w_rows, 1, 1).astype(BF16).reshape(w.shape)
        o = lax.dot_general(w_odd, x, (((2,), (1,)), ((0,), (0,))), preferred_element_type=F32)
        o = o + w_new.astype(BF16).astype(F32) * newv_ref[kv]
        o = o / total
        for r in range(R):
            col = (kv * R + r) * HEAD_WIDTH
            att_all[u_me, 0:NS, col:col + HEAD_WIDTH] = o[:, r, :].astype(BF16)
    at_copies = []
    for d in range(1, U):
        at_copies.append(
            send(att_all.at[u_me], att_all.at[u_me], at_s.at[d], at_r.at[d],
                 {"sub": lax.rem(u_me + d, U)})
        )
    for c in at_copies:
        c.wait_recv()
    loads[0].wait()
    M = U * NR
    att = att_all[...].reshape(M, att_all.shape[2])
    parts[t_me] = jnp.dot(att, wo[...], preferred_element_type=F32).astype(BF16)
    pa_copies = []
    for d in range(1, T):
        pa_copies.append(
            send(parts.at[t_me], parts.at[t_me], pa_s.at[d], pa_r.at[d],
                 {"tensor": lax.rem(t_me + d, T)})
        )
    for c in st_copies:
        c.wait_recv()

    def arrange(c, _):
        row = strecv[order_ref[c]]
        gath[p_me, c] = row
        n29[pl.ds(c, 1), :] = row.astype(F32)[last:last + 1, :]
        return 0

    lax.fori_loop(0, SL, arrange, 0)
    for c in pa_copies:
        c.wait_recv()
    g_copies = []
    for d in range(1, NP):
        g_copies.append(send(gath.at[p_me], gath.at[p_me], g_s.at[d], g_r.at[d], at_part(d)))
    mixing = parts[0].astype(F32)
    for t in range(1, T):
        mixing = mixing + parts[t].astype(F32)
    hidden = (resid_ref[...].astype(F32) + mixing).astype(BF16)
    hid_ref[...] = hidden
    wide = hidden.astype(F32)
    gained = (wide * gain_ref[...]).astype(BF16)
    loads[1].wait()
    AW = adapt.shape[1]
    condx[u_me, :, 0:AW] = jnp.dot(gained, adapt[...], preferred_element_type=F32)
    condx[u_me, :, AW:AW + 128] = jnp.broadcast_to(
        jnp.sum(wide * wide, axis=-1, keepdims=True), (M, 128)
    )
    cx_copies = []
    for d in range(1, U):
        cx_copies.append(
            send(condx.at[u_me], condx.at[u_me], cx_s.at[d], cx_r.at[d],
                 {"sub": lax.rem(u_me + d, U)})
        )
    condpack[...] = jnp.zeros(condpack.shape, F32)
    for c in cx_copies:
        c.wait_recv()
    mine = pl.ds(pl.multiple_of(u_me * CW, 128), CW)
    acc, sq = condx[0, :, mine], condx[0, :, AW:AW + 128]
    for u in range(1, U):
        acc = acc + condx[u, :, mine]
        sq = sq + condx[u, :, AW:AW + 128]
    inv = lax.rsqrt(sq[:, 0:1] / (hidden.shape[1] * U) + epsilon)
    condf[...] = acc * inv

    def pack_cond(o, _):
        for r in range(SLOTS):
            condpack[pl.ds(o * 16 + r, 1), :] = condf[pl.ds(crow_ref[o * SLOTS + r], 1), :]
        return 0

    lax.fori_loop(0, S, pack_cond, 0)
    condsend[...] = condpack[...].astype(BF16).reshape(condsend.shape)
    co_copies = []
    for d in range(1, S):
        o = lax.rem(me + d, S)
        co_copies.append(
            send(condsend.at[o], condrecv.at[me], co_s.at[d], co_r.at[d], at_stream(d))
        )
    condrecv[me] = condsend[me]
    lgf[...] = jnp.zeros(lgf.shape, F32)
    for c in co_copies:
        c.wait_recv()
    condrf[...] = condrecv[...].astype(F32).reshape(condrf.shape)

    def last_rows(c, _):
        lgf[p_me, pl.ds(c, 1), :] = n29[pl.ds(c, 1), :] + condrf[pl.ds(orow_ref[c], 1), :]
        return 0

    lax.fori_loop(0, SL, last_rows, 0)
    lg[p_me] = lgf[p_me].astype(BF16)
    l_copies = []
    for d in range(1, NP):
        l_copies.append(send(lg.at[p_me], lg.at[p_me], l_s.at[d], l_r.at[d], at_part(d)))
    for c in g_copies:
        c.wait_recv()
    for c in l_copies:
        c.wait_recv()
    lgf[...] = lg[...].astype(F32)

    is_last = lax.broadcasted_iota(jnp.int32, (TOK, CW), 0) == last

    def full_rows(part, c):
        return jnp.where(is_last, lgf[part, pl.ds(c, 1), :], gath[part, c].astype(F32))

    def normalize(c, _):
        rows = [full_rows(pt, c) for pt in range(NP)]
        ss = rows[0] * rows[0]
        for x in rows[1:]:
            ss = ss + x * x
        inv = lax.rsqrt(jnp.sum(ss, axis=-1, keepdims=True) / (NP * CW) + epsilon)
        for pt in range(NP):
            a_s[c, :, pt * CW:(pt + 1) * CW] = (
                rows[pt] * inv * dgain_ref[:, pt * CW:(pt + 1) * CW]
            ).astype(BF16)
        return 0

    lax.fori_loop(0, SL, normalize, 0)
    loads[2].wait()
    loads[3].wait()

    def project(p, _):
        here = pl.ds(p * SLOTS, SLOTS)
        a = a_s[here].reshape(SLOTS * TOK, NP * CW)
        for k, dst in enumerate((qb, kb, vb)):
            y = jnp.dot(a, qkv[k], preferred_element_type=F32)
            if k == 0:
                y = y * (DHD ** (-0.5))
            dst[here] = y.astype(BF16).reshape(SLOTS, TOK, CW)
        return 0

    lax.fori_loop(0, S, project, 0)

    H = CW // DHD
    lane = lax.broadcasted_iota(jnp.int32, (1, CW), 1)
    heads = [(lane // DHD == h).astype(F32) for h in range(H)]
    heads_b = [m.astype(BF16) for m in heads]
    XR = crecv.shape[1]
    key_lane = lax.broadcasted_iota(jnp.int32, (1, XR), 1)
    past = 2 * past_len
    bias_c = jnp.where((key_lane % 2 == 0) & (key_lane < past), 0.0, NEG)
    bias_o = jnp.where(lax.broadcasted_iota(jnp.int32, (1, TOK), 1) <= last, 0.0, NEG)

    o_copies = []
    for d in range(S):
        p = lax.rem(me - d + S, S)
        if d > 0:
            ca_copies[d].wait_recv()

        def attend(k, _):
            c = p * SLOTS + k
            q = qb[c]
            qs = jnp.concatenate([q * m for m in heads_b], axis=0)
            x = crecv[c]
            s = dot_nt(qs, x) + bias_c
            so = dot_nt(qs, kb[c]) + bias_o
            top = jnp.maximum(
                jnp.max(s, axis=-1, keepdims=True), jnp.max(so, axis=-1, keepdims=True)
            )
            w = jnp.exp(s - top)
            w_own = jnp.exp(so - top)
            total = jnp.sum(w, axis=-1, keepdims=True) + jnp.sum(w_own, axis=-1, keepdims=True)
            y = jnp.dot(pltpu.roll(w, 1, 1).astype(BF16), x, preferred_element_type=F32)
            y = y + jnp.dot(w_own.astype(BF16), vb[c], preferred_element_type=F32)
            y = y / total
            m = y[0:TOK] * heads[0]
            for h in range(1, H):
                m = m + y[h * TOK:(h + 1) * TOK] * heads[h]
            mx[pl.ds(pl.multiple_of(k * TOK, TOK), TOK), :] = m.astype(BF16)
            return 0

        lax.fori_loop(0, SLOTS, attend, 0, unroll=True)
        for e in range(NP):
            pt = lax.rem(p_me + e, NP)
            y = jnp.dot(
                mx[...], dout[:, pl.ds(pl.multiple_of(pt * CW, 128), CW)],
                preferred_element_type=F32,
            )
            if e == 0:
                own[d] = y
            else:
                osend[e, d] = y.astype(BF16)
                o_copies.append(
                    send(osend.at[e, d], orecv.at[e, d], o_s.at[e, d], o_r.at[e, d], at_part(e))
                )
    i = 0
    for d in range(S):
        p = lax.rem(me - d + S, S)
        mix = own[d]
        for e in range(1, NP):
            o_copies[i].wait_recv()
            mix = mix + orecv[e, d].astype(F32)
            i += 1
        mix = mix.reshape(SLOTS, TOK, CW)
        for k in range(SLOTS):
            c = p * SLOTS + k
            x = full_rows(p_me, c)
            res[c] = step_size * (x + mix[k])

    def write(qn, _):
        y = res[outidx_ref[qn]] * live_ref[qn].astype(F32)
        out_ref[qn] = y[0:last + 1, :].astype(BF16)
        return 0

    lax.fori_loop(0, SL, write, 0)
    for c in (st_copies + ca_copies[1:] + at_copies + pa_copies + g_copies + cx_copies
              + co_copies + l_copies + o_copies):
        c.wait_send()


def exclusive_rank(hot, axis):
    return jnp.sum((jnp.cumsum(hot, axis=axis) - hot) * hot, axis=-1)


def routing(complete, owner, prev_owner, S, SH, home, NS, NR):
    n = owner.shape[0]
    rng = jnp.arange(S)
    done = complete == 1
    owner_hot = ((owner[:, None] == rng[None, :]) & done[:, None]).astype(jnp.int32)
    by_home = owner_hot.reshape(S, SH, S)
    home_rank = jnp.sum(
        (jnp.cumsum(by_home, axis=1) - by_home).reshape(n, S) * owner_hot, axis=-1
    )
    prev_hot = (prev_owner[:, None] == rng[None, :]).astype(jnp.int32)
    cache_slot = exclusive_rank(prev_hot, 0)
    pair = prev_owner * S + owner
    pair_hot = ((pair[:, None] == jnp.arange(S * S)[None, :]) & done[:, None]).astype(jnp.int32)
    pair_rank = exclusive_rank(pair_hot, 0)
    ids = jnp.arange(n)
    shard = ids // SH
    local = ids - shard * SH
    slots = jnp.arange(S * SLOTS)

    def pick(valid, slot, value):
        hot = (slots[:, None] == slot[None, :]) & valid[None, :]
        return jnp.sum(jnp.where(hot, value[None, :], 0), axis=1).astype(jnp.int32), hot

    pack, _ = pick(done & (shard == home), owner * SLOTS + home_rank, local)
    cpack, _ = pick(done & (prev_owner == home), owner * SLOTS + pair_rank, cache_slot)
    crow = pack // NS * NR + pack % NS
    owned = done & (owner == home)
    home_slot = shard * SLOTS + home_rank
    cache_order = prev_owner * SLOTS + pair_rank
    order, _ = pick(owned, cache_order, home_slot)
    orow = order // SLOTS * 16 + order % SLOTS
    outidx, hot = pick(owned, home_slot, cache_order)
    live = jnp.sum(hot.astype(jnp.int32), axis=1)
    return pack, cpack, crow, order, orow, outidx, live


def shards(
    lm_query, lm_cache, language_new_pair, lm_lengths, lm_resid, lm_wo, lm_gain, lm_adapt,
    det_noise, det_pending, det_cache, det_qkv, det_out, det_gain, complete, owner, prev_owner,
):
    S, T, U = lax.axis_size("stream"), lax.axis_size("tensor"), lax.axis_size("sub")
    NP = T * U
    home = lax.axis_index("stream")
    NS = lm_query.shape[0]
    SH = NS * U
    NR = up(NS, 16)
    M = U * NR
    QW = lm_query.shape[1]
    KV = lm_cache.shape[-1] // HEAD_WIDTH
    R = QUERY_HEADS // KEY_VALUE_HEADS
    span = det_noise.shape[1]
    CW = det_noise.shape[2]
    TOK = up(span, 16)
    past = det_cache.shape[2]
    XR = up(2 * past, 128)
    SL = S * SLOTS
    CL = up(SL, 16)
    HID = lm_resid.shape[1]
    AW = lm_adapt.shape[1]

    tables = routing(complete, owner, prev_owner, S, SH, home, NS, NR)
    first = (home * U + lax.axis_index("sub")) * NS
    lengths = lax.dynamic_slice_in_dim(lm_lengths, first, NS, 0)
    LR = 2 * lm_cache.shape[1]
    lanes = jnp.arange(LR)
    bias = jnp.where(
        (lanes % 2 == 0)[None, :] & (lanes[None, :] < 2 * lengths[:, None]), 0.0, NEG
    ).astype(F32)[:, None, :]
    q = jnp.transpose(lm_query.reshape(NS, KV, R, HEAD_WIDTH), (1, 0, 2, 3))
    q = jnp.pad(q, ((0, 0), (0, 0), (0, 8 - R), (0, 0)))
    lmx = lm_cache.reshape(NS, LR, KV * HEAD_WIDTH)
    pair = jnp.transpose(
        language_new_pair.astype(F32).reshape(NS, 2, KV, HEAD_WIDTH), (1, 2, 0, 3)
    )[:, :, :, None, :]
    resid = jnp.pad(lm_resid.reshape(U, NS, HID), ((0, 0), (0, NR - NS), (0, 0))).reshape(M, HID)
    state = (
        det_noise.astype(F32) + jnp.pad(det_pending, ((0, 0), (0, 1), (0, 0))).astype(F32)
    ).astype(BF16)
    state = jnp.pad(state, ((0, 0), (0, TOK - span), (0, 0)))
    dcache = jnp.pad(
        det_cache.reshape(SH, 2 * past, CW), ((0, 0), (0, XR - 2 * past), (0, 0))
    )
    sizes = (S, T, U)
    V = pl.BlockSpec(memory_space=pltpu.VMEM)
    SM = pl.BlockSpec(memory_space=pltpu.SMEM)
    ANY = pl.BlockSpec(memory_space=pl.ANY)
    v = pltpu.VMEM
    dma = pltpu.SemaphoreType.DMA
    scratch = [
        v(lm_wo.shape, BF16), v(lm_adapt.shape, BF16), v(det_qkv.shape, BF16),
        v(det_out.shape, BF16),
        v((SL, TOK, CW), BF16), v((SL, TOK, CW), BF16),
        v((SL, XR, CW), BF16), v((SL, XR, CW), BF16),
        v((U, NR, QW), BF16), v((T, M, HID), BF16), v((U, M, AW + 128), F32),
        v((M, CW), F32), v((S * 16, CW), F32), v((S, 16, CW), BF16), v((S, 16, CW), BF16),
        v((S * 16, CW), F32), v((NP, SL, TOK, CW), BF16), v((CL, CW), F32),
        v((NP, CL, CW), BF16), v((NP, CL, CW), F32), v((SL, TOK, NP * CW), BF16),
        v((SL, TOK, CW), BF16), v((SL, TOK, CW), BF16), v((SL, TOK, CW), BF16),
        v((SLOTS * TOK, CW), BF16), v((S, SLOTS * TOK, CW), F32),
        v((NP, S, SLOTS * TOK, CW), BF16), v((NP, S, SLOTS * TOK, CW), BF16),
        v((SL, TOK, CW), F32),
        dma((4,)), dma((S,)), dma((S,)), dma((S,)), dma((S,)), dma((S,)), dma((S,)),
        dma((U,)), dma((U,)), dma((T,)), dma((T,)), dma((U,)), dma((U,)),
        dma((NP,)), dma((NP,)), dma((NP,)), dma((NP,)), dma((NP, S)), dma((NP, S)),
    ]
    hidden, new_state = pl.pallas_call(
        functools.partial(kernel, sizes, past),
        out_shape=(
            jax.ShapeDtypeStruct((M, HID), BF16),
            jax.ShapeDtypeStruct((SL, span, CW), BF16),
        ),
        in_specs=[SM] * 7 + [V] * 10 + [ANY] * 4,
        out_specs=(V, V),
        scratch_shapes=scratch,
        compiler_params=pltpu.CompilerParams(
            collective_id=0, has_side_effects=True, vmem_limit_bytes=60 * 1024 * 1024
        ),
    )(
        *tables, state, dcache, q, lmx, pair[0], pair[1], bias, resid,
        lm_gain.astype(F32)[None, :], det_gain.astype(F32)[None, :],
        lm_wo, lm_adapt, det_qkv, det_out,
    )
    hidden = hidden.reshape(U, NR, HID)[:, :NS].reshape(SH, HID)
    return hidden, new_state.reshape(1, S, SLOTS, span, CW)


def solution(mesh):
    return jax.shard_map(
        shards,
        mesh=mesh,
        in_specs=(
            P(("groups", "stream", "sub"), "tensor"),
            P(("groups", "stream", "sub"), None, None, "tensor"),
            P(("groups", "stream", "sub"), None, "tensor"),
            P("groups"),
            P(("groups", "stream"), "sub"),
            P("tensor", "sub"),
            P("sub"),
            P("sub", "tensor"),
            P(("groups", "stream"), None, ("tensor", "sub")),
            P(("groups", "stream"), None, ("tensor", "sub")),
            P(("groups", "stream"), None, None, None, ("tensor", "sub")),
            P(None, None, ("tensor", "sub")),
            P(("tensor", "sub"), None),
            P(),
            P("groups"),
            P("groups"),
            P("groups"),
        ),
        out_specs=(
            P(("groups", "stream"), "sub"),
            P(("groups", "stream"), None, None, None, ("tensor", "sub")),
        ),
        check_vma=False,
    )
```

profile of v0, /device:TPU:0, one launch (start us, length us, event | category | flops | bytes accessed | tf_op | source)
XLA Modules:
  0.0 103.8 jit_solution(15721707486742625209)
XLA Ops:
  0.6 0.7 compare_and_fusion
  1.4 0.7 eq.129
  2.6 0.7 multiply_add_fusion.2
  3.7 0.7 multiply_add_fusion.1
  4.4 0.7 fusion
  5.3 0.8 select_reduce_fusion
  6.1 0.7 select_reduce_fusion.3
  6.9 0.6 fusion.10.orow_ref
  7.6 0.5 fusion.9.crow_ref
  8.1 0.7 dynamic-slice_multiply_fusion
  8.9 0.7 and_select_fusion.bias_ref
  9.6 0.7 bitcast_bitcast_fusion
  10.3 0.6 slice_bitcast_fusion
  10.9 3.5 %reshape.171 = bf16[24,120,256]{2,1,0:T(8,128)(2,1)S(1)} reshape(bf16[1,24,60,2,256]{4,3,2,1,0:T(2,128)(2,1)} %param.27) | data formatting | bytes 2949120 | tf_op jit(solution)/shard_map/reshape | solution.py:435
  14.4 1.3 %pad.22.dcache_ref = bf16[24,128,256]{2,1,0:T(8,128)(2,1)} pad(bf16[24,120,256]{2,1,0:T(8,128)(2,1)S(1)} %reshape.171, bf16[]{:T(256)} %constant.87.clone.1), padding=0_0x0_8x0_0 | pad | bytes 3047426 | tf_op jit(solution)/shard_map/jit(_pad)/pad | solution.py:434
  16.1 0.8 pad.21.state_ref
  16.9 1.2 %reshape.173.lmx_ref = bf16[12,128,256]{2,1,0:T(8,128)(2,1)} reshape(bf16[12,64,2,256]{3,2,1,0:T(2,128)(2,1)S(1)} %copy-done) | data formatting | bytes 1572864 | tf_op jit(solution)/shard_map/reshape | solution.py:425
  18.1 0.7 pad.24
  18.9 0.6 pad.23.q_ref
  19.5 0.6 reshape.180.gain_ref
  20.1 0.6 broadcast_in_dim.86
  20.7 79.5 %shard_map.176 = (bf16[32,1792]{1,0:T(8,128)(2,1)}, bf16[24,30,256]{2,1,0:T(8,128)(2,1)}) custom-call(s32[24]{0:T(128)} %copy-done.7, s32[24]{0:T(128)} %get-tuple-element.25.cpack_ref, s32[24]{0:T(128)} %fusion.9.crow_ref, s32[24]{0:T(128)} %copy-done.6, s32[24]{0:T(128)} %fusion.10.orow_ref, s32[24]{0:T(128)} %get-tuple-element.12.outidx_ref, ...), custom_call_target="tpu_custom_call" | custom-call | tf_op jit(solution)/shard_map/pallas_call | solution.py:460
  100.2 2.0 %copy.31 = bf16[1,4,6,30,256]{4,1,3,2,0:T(4,128)(2,1)} copy(bf16[1,4,6,30,256]{4,3,2,1,0:T(8,128)(2,1)} %bitcast.20) | data formatting | bytes 737280
  102.2 1.6 %reshape.178 = bf16[24,1792]{1,0:T(8,128)(2,1)} reshape(bf16[2,12,1792]{2,1,0:T(8,128)(2,1)} %bitcast.22) | data formatting | bytes 172032 | tf_op jit(solution)/shard_map/reshape | solution.py:477
  (35 shorter events, 1.7 us)
Async XLA Ops:
  6.9 8.9 %copy-start.6 = (s32[24]{0:T(128)}, s32[24]{0:T(128)S(1)}, u32[]{:S(2)}) copy-start(s32[24]{0:T(128)S(1)} %get-tuple-element.13.order_ref) | copy-start | bytes 292
  7.6 8.2 %copy-start.7 = (s32[24]{0:T(128)}, s32[24]{0:T(128)S(1)}, u32[]{:S(2)}) copy-start(s32[24]{0:T(128)S(1)} %select_reduce_fusion.6.pack_ref) | copy-start | bytes 292
  14.4 1.4 %copy-start.2 = (bf16[24,29,256]{2,0,1:T(8,128)(2,1)S(1)}, bf16[24,29,256]{2,0,1:T(8,128)(2,1)}, u32[]{:S(2)}) copy-start(bf16[24,29,256]{2,0,1:T(8,128)(2,1)} %param.26) | copy-start | bytes 1069060
  14.4 1.5 %copy-start.1 = (bf16[24,30,256]{2,0,1:T(8,128)(2,1)S(1)}, bf16[24,30,256]{2,0,1:T(8,128)(2,1)}, u32[]{:S(2)}) copy-start(bf16[24,30,256]{2,0,1:T(8,128)(2,1)} %param.25) | copy-start | bytes 1105924
  15.8 1.1 %copy-start = (bf16[12,64,2,256]{3,2,1,0:T(2,128)(2,1)S(1)}, bf16[12,64,2,256]{3,2,1,0:T(2,128)(2,1)}, u32[]{:S(2)}) copy-start(bf16[12,64,2,256]{3,2,1,0:T(2,128)(2,1)} %param.18) | copy-start | bytes 2359300
  15.9 2.2 %copy-start.3 = (bf16[24,1792]{1,0:T(8,128)(2,1)S(1)}, bf16[24,1792]{1,0:T(8,128)(2,1)}, u32[]{:S(2)}) copy-start(bf16[24,1792]{1,0:T(8,128)(2,1)} %param.21) | copy-start | bytes 258052
  16.0 2.8 %copy-start.4 = (bf16[12,1792]{1,0:T(8,128)(2,1)S(1)}, bf16[12,1792]{1,0:T(8,128)(2,1)}, u32[]{:S(2)}) copy-start(bf16[12,1792]{1,0:T(8,128)(2,1)} %param.17) | copy-start | bytes 129028
  16.0 3.5 %copy-start.5 = (bf16[1792]{0:T(1024)(128)(2,1)S(1)}, bf16[1792]{0:T(1024)(128)(2,1)}, u32[]{:S(2)}) copy-start(bf16[1792]{0:T(1024)(128)(2,1)} %param.23) | copy-start | bytes 10756
  16.1 4.1 %copy-start.8 = (bf16[1024]{0:T(1024)(128)(2,1)S(1)}, bf16[1024]{0:T(1024)(128)(2,1)}, u32[]{:S(2)}) copy-start(bf16[1024]{0:T(1024)(128)(2,1)} %param.30) | copy-start | bytes 6148
where the time goes:
time: 105 us; the launch traced here: 104 us
  Pallas kernels  79.5 us (76%)
  local copies, waits for them, and re-layouts  14.1 us (13%)
  other arithmetic  9.41 us (9%)
    pallas_call x1, Pallas kernels, shards(): pl.pallas_call(functools.partial(kernel, sizes, past), out_shape=(jax.Sha...  79.5 us
    reshape x1, local copies, waits for them, and re-layouts, shards(): det_cache.reshape(SH, 2 * past, CW)  3.49 us
    unnamed x20, local copies, waits for them, and re-layouts  2.21 us

commit v1 on v0

--- a/solution.py
+++ b/solution.py
@@ -32,27 +32,25 @@
 def kernel(
     sizes,
     past_len,
-    pack_ref, cpack_ref, crow_ref, order_ref, orow_ref, outidx_ref, live_ref,
-    state_ref, dcache_ref, q_ref, lmx_ref, newk_ref, newv_ref, bias_ref, resid_ref, gain_ref,
-    dgain_ref,
+    tab_ref, len_ref,
+    noise_ref, pend_ref, dcache_ref, query_ref, lmx_ref, pair_ref, resid_ref, gain_ref, dgain_ref,
     wo_hbm, adapt_hbm, qkv_hbm, dout_hbm,
     hid_ref, out_ref,
-    wo, adapt, qkv, dout,
+    wo, adapt, qkv, dout, bias_s, q_s, resid_s,
     stsend, strecv, csend, crecv, att_all, parts, condx, condf, condpack, condsend, condrecv,
     condrf, gath, n29, lg, lgf, a_s, qb, kb, vb, mx, own, osend, orecv, res,
     w_sem, st_s, st_r, ca_s, ca_r, co_s, co_r, at_s, at_r, pa_s, pa_r, cx_s, cx_r,
     g_s, g_r, l_s, l_r, o_s, o_r,
 ):
     S, T, U = sizes
+    past = 2 * past_len
     NP = T * U
     me = lax.axis_index("stream")
     t_me = lax.axis_index("tensor")
     u_me = lax.axis_index("sub")
     p_me = t_me * U + u_me
-    CW = state_ref.shape[2]
-    TOK = state_ref.shape[1]
-    SL = S * SLOTS
-    KV, NS = q_ref.shape[0], q_ref.shape[1]
+    SL, TOK, CW = stsend.shape
+    KV, NS = q_s.shape[0], q_s.shape[1]
     NR = att_all.shape[1]
     R = QUERY_HEADS // KEY_VALUE_HEADS
     last = out_ref.shape[1] - 1
@@ -85,7 +83,11 @@
         pl.semaphore_signal(barrier, inc=1, device_id=at_part(d), device_id_type=MESH)
 
     def pack_state(i, _):
-        stsend[i] = state_ref[pack_ref[i]]
+        k = tab_ref[0, i]
+        pend = jnp.concatenate([pend_ref[k].astype(F32), jnp.zeros((1, CW), F32)], axis=0)
+        row = noise_ref[k].astype(F32) + pend
+        row = jnp.concatenate([row, jnp.zeros((TOK - last - 1, CW), F32)], axis=0)
+        stsend[i] = row.astype(BF16)
         return 0
 
     lax.fori_loop(0, SL, pack_state, 0)
@@ -98,19 +100,27 @@
                  st_s.at[d], st_r.at[d], at_stream(d))
         )
 
+    if past < csend.shape[1]:
+        csend[:, past:] = jnp.zeros((SL, csend.shape[1] - past, CW), BF16)
+
     def pack_cache(i, _):
-        csend[i] = dcache_ref[cpack_ref[i]]
+        row = dcache_ref[tab_ref[1, i]].reshape(past, CW)
+        csend[i, 0:past] = row
         return 0
 
     lax.fori_loop(0, SL, pack_cache, 0)
     ca_copies = [None]
-    for d in range(1, S):
+
+    def send_cache(d):
         o = lax.rem(me + d, S)
         ca_copies.append(
             send(csend.at[pl.ds(o * SLOTS, SLOTS)], crecv.at[pl.ds(me * SLOTS, SLOTS)],
                  ca_s.at[d], ca_r.at[d], at_stream(d))
         )
 
+    for d in range(1, S // 2):
+        send_cache(d)
+
     def keep_own(i, _):
         c = me * SLOTS + i
         strecv[c] = stsend[c]
@@ -120,15 +130,32 @@
     lax.fori_loop(0, SLOTS, keep_own, 0)
 
     scale = HEAD_WIDTH ** (-0.5)
-    bias = bias_ref[...]
+    LR = bias_s.shape[2]
+    lane_l = lax.broadcasted_iota(jnp.int32, (1, LR), 1)
+    first = (me * U + u_me) * NS
+    for i in range(NS):
+        seen = (lane_l % 2 == 0) & (lane_l < 2 * len_ref[first + i])
+        bias_s[i] = jnp.where(seen, 0.0, NEG)
+    bias = bias_s[...]
+    q_s[...] = jnp.zeros(q_s.shape, F32)
+    for h in range(KV * R):
+        q_s[h // R, :, h % R, :] = query_ref[
+            :, h * HEAD_WIDTH:(h + 1) * HEAD_WIDTH
+        ].astype(F32)
+    if NR > NS:
+        resid_s[...] = jnp.zeros(resid_s.shape, F32)
+    for u in range(U):
+        resid_s[u * NR:u * NR + NS] = resid_ref[...].astype(F32)[u * NS:(u + 1) * NS]
+    pair = pair_ref[...].astype(F32)
     if NR > NS:
         att_all[u_me] = jnp.zeros(att_all.shape[1:], BF16)
     for kv in range(KV):
-        q = q_ref[kv]
+        q = q_s[kv]
+        pair_kv = pair[:, :, kv * HEAD_WIDTH:(kv + 1) * HEAD_WIDTH]
         x = lmx_ref[:, :, kv * HEAD_WIDTH:(kv + 1) * HEAD_WIDTH]
-        s = lax.dot_general(q, x, (((2,), (2,)), ((0,), (0,))), preferred_element_type=F32)
+        s = lax.dot_general(q.astype(BF16), x, (((2,), (2,)), ((0,), (0,))), preferred_element_type=F32)
         s = s * scale + bias
-        s_new = jnp.sum(q.astype(F32) * newk_ref[kv], axis=-1, keepdims=True) * scale
+        s_new = jnp.sum(q * pair_kv[:, 0:1], axis=-1, keepdims=True) * scale
         top = jnp.maximum(jnp.max(s, axis=-1, keepdims=True), s_new)
         w = jnp.exp(s - top)
         w_new = jnp.exp(s_new - top)
@@ -136,7 +163,7 @@
         w_rows = w.reshape(NS * 8, w.shape[2])
         w_odd = pltpu.roll(w_rows, 1, 1).astype(BF16).reshape(w.shape)
         o = lax.dot_general(w_odd, x, (((2,), (1,)), ((0,), (0,))), preferred_element_type=F32)
-        o = o + w_new.astype(BF16).astype(F32) * newv_ref[kv]
+        o = o + w_new.astype(BF16).astype(F32) * pair_kv[:, 1:2]
         o = o / total
         for r in range(R):
             col = (kv * R + r) * HEAD_WIDTH
@@ -163,7 +190,7 @@
         c.wait_recv()
 
     def arrange(c, _):
-        row = strecv[order_ref[c]]
+        row = strecv[tab_ref[3, c]]
         gath[p_me, c] = row
         n29[pl.ds(c, 1), :] = row.astype(F32)[last:last + 1, :]
         return 0
@@ -177,10 +204,11 @@
     mixing = parts[0].astype(F32)
     for t in range(1, T):
         mixing = mixing + parts[t].astype(F32)
-    hidden = (resid_ref[...].astype(F32) + mixing).astype(BF16)
-    hid_ref[...] = hidden
+    hidden = (resid_s[...] + mixing).astype(BF16)
+    for u in range(U):
+        hid_ref[u * NS:(u + 1) * NS] = hidden[u * NR:u * NR + NS]
     wide = hidden.astype(F32)
-    gained = (wide * gain_ref[...]).astype(BF16)
+    gained = (wide * gain_ref[...].astype(F32)).astype(BF16)
     loads[1].wait()
     AW = adapt.shape[1]
     condx[u_me, :, 0:AW] = jnp.dot(gained, adapt[...], preferred_element_type=F32)
@@ -206,7 +234,7 @@
 
     def pack_cond(o, _):
         for r in range(SLOTS):
-            condpack[pl.ds(o * 16 + r, 1), :] = condf[pl.ds(crow_ref[o * SLOTS + r], 1), :]
+            condpack[pl.ds(o * 16 + r, 1), :] = condf[pl.ds(tab_ref[2, o * SLOTS + r], 1), :]
         return 0
 
     lax.fori_loop(0, S, pack_cond, 0)
@@ -217,6 +245,8 @@
         co_copies.append(
             send(condsend.at[o], condrecv.at[me], co_s.at[d], co_r.at[d], at_stream(d))
         )
+    for d in range(max(1, S // 2), S):
+        send_cache(d)
     condrecv[me] = condsend[me]
     lgf[...] = jnp.zeros(lgf.shape, F32)
     for c in co_copies:
@@ -224,7 +254,7 @@
     condrf[...] = condrecv[...].astype(F32).reshape(condrf.shape)
 
     def last_rows(c, _):
-        lgf[p_me, pl.ds(c, 1), :] = n29[pl.ds(c, 1), :] + condrf[pl.ds(orow_ref[c], 1), :]
+        lgf[p_me, pl.ds(c, 1), :] = n29[pl.ds(c, 1), :] + condrf[pl.ds(tab_ref[4, c], 1), :]
         return 0
 
     lax.fori_loop(0, SL, last_rows, 0)
@@ -242,6 +272,8 @@
 
     def full_rows(part, c):
         return jnp.where(is_last, lgf[part, pl.ds(c, 1), :], gath[part, c].astype(F32))
+
+    dgain = dgain_ref[...].astype(F32)
 
     def normalize(c, _):
         rows = [full_rows(pt, c) for pt in range(NP)]
@@ -251,7 +283,7 @@
         inv = lax.rsqrt(jnp.sum(ss, axis=-1, keepdims=True) / (NP * CW) + epsilon)
         for pt in range(NP):
             a_s[c, :, pt * CW:(pt + 1) * CW] = (
-                rows[pt] * inv * dgain_ref[:, pt * CW:(pt + 1) * CW]
+                rows[pt] * inv * dgain[:, pt * CW:(pt + 1) * CW]
             ).astype(BF16)
         return 0
 
@@ -277,7 +309,6 @@
     heads_b = [m.astype(BF16) for m in heads]
     XR = crecv.shape[1]
     key_lane = lax.broadcasted_iota(jnp.int32, (1, XR), 1)
-    past = 2 * past_len
     bias_c = jnp.where((key_lane % 2 == 0) & (key_lane < past), 0.0, NEG)
     bias_o = jnp.where(lax.broadcasted_iota(jnp.int32, (1, TOK), 1) <= last, 0.0, NEG)
 
@@ -338,7 +369,7 @@
             res[c] = step_size * (x + mix[k])
 
     def write(qn, _):
-        y = res[outidx_ref[qn]] * live_ref[qn].astype(F32)
+        y = res[tab_ref[5, qn]] * tab_ref[6, qn].astype(F32)
         out_ref[qn] = y[0:last + 1, :].astype(BF16)
         return 0
 
@@ -348,44 +379,54 @@
         c.wait_send()
 
 
-def exclusive_rank(hot, axis):
-    return jnp.sum((jnp.cumsum(hot, axis=axis) - hot) * hot, axis=-1)
-
-
-def routing(complete, owner, prev_owner, S, SH, home, NS, NR):
-    n = owner.shape[0]
-    rng = jnp.arange(S)
-    done = complete == 1
-    owner_hot = ((owner[:, None] == rng[None, :]) & done[:, None]).astype(jnp.int32)
-    by_home = owner_hot.reshape(S, SH, S)
-    home_rank = jnp.sum(
-        (jnp.cumsum(by_home, axis=1) - by_home).reshape(n, S) * owner_hot, axis=-1
-    )
-    prev_hot = (prev_owner[:, None] == rng[None, :]).astype(jnp.int32)
-    cache_slot = exclusive_rank(prev_hot, 0)
-    pair = prev_owner * S + owner
-    pair_hot = ((pair[:, None] == jnp.arange(S * S)[None, :]) & done[:, None]).astype(jnp.int32)
-    pair_rank = exclusive_rank(pair_hot, 0)
-    ids = jnp.arange(n)
+def routing_kernel(dims, done_ref, owner_ref, prev_ref, tab_ref):
+    S, SH, NS, NR = dims
+    n = done_ref.shape[1]
+    home = lax.axis_index("stream")
+    done = done_ref[...] == 1
+    owner = owner_ref[...]
+    prev = prev_ref[...]
+    before = lax.broadcasted_iota(jnp.int32, (n, n), 0)
+    after = lax.broadcasted_iota(jnp.int32, (n, n), 1)
+    earlier = (before < after).astype(F32)
+    same = jnp.where(before // SH == after // SH, earlier, 0.0).astype(BF16)
+    earlier = earlier.astype(BF16)
+
+    def rank(key, count, valid, order):
+        rows = lax.broadcasted_iota(jnp.int32, (count, n), 0)
+        hot = jnp.where((rows == key) & valid, 1.0, 0.0)
+        cum = jnp.dot(hot.astype(BF16), order, preferred_element_type=F32)
+        return jnp.sum(cum * hot, axis=0, keepdims=True)
+
+    always = owner >= 0
+    home_rank = rank(owner, S, done, same)
+    cache_slot = rank(prev, S, always, earlier)
+    pair_rank = rank(prev * S + owner, S * S, done, earlier).astype(jnp.int32)
+    ids = lax.broadcasted_iota(jnp.int32, (1, n), 1)
     shard = ids // SH
-    local = ids - shard * SH
-    slots = jnp.arange(S * SLOTS)
+    local = (ids - shard * SH).astype(F32)
+    home_slot = shard * SLOTS + home_rank.astype(jnp.int32)
+    target = owner * SLOTS + home_rank.astype(jnp.int32)
+    cache_order = prev * SLOTS + pair_rank
+    width = tab_ref.shape[1]
+    slots = lax.broadcasted_iota(jnp.int32, (width, n), 0)
 
     def pick(valid, slot, value):
-        hot = (slots[:, None] == slot[None, :]) & valid[None, :]
-        return jnp.sum(jnp.where(hot, value[None, :], 0), axis=1).astype(jnp.int32), hot
-
-    pack, _ = pick(done & (shard == home), owner * SLOTS + home_rank, local)
-    cpack, _ = pick(done & (prev_owner == home), owner * SLOTS + pair_rank, cache_slot)
-    crow = pack // NS * NR + pack % NS
+        hot = jnp.where((slots == slot) & valid, 1.0, 0.0).astype(BF16)
+        value = jnp.broadcast_to(value, (8, n)).astype(BF16)
+        return dot_nt(value, hot)[0:1].astype(jnp.int32)
+
+    pack = pick(done & (shard == home), target, local)
     owned = done & (owner == home)
-    home_slot = shard * SLOTS + home_rank
-    cache_order = prev_owner * SLOTS + pair_rank
-    order, _ = pick(owned, cache_order, home_slot)
-    orow = order // SLOTS * 16 + order % SLOTS
-    outidx, hot = pick(owned, home_slot, cache_order)
-    live = jnp.sum(hot.astype(jnp.int32), axis=1)
-    return pack, cpack, crow, order, orow, outidx, live
+    order = pick(owned, cache_order, home_slot.astype(F32))
+    tab_ref[0:1] = pack
+    tab_ref[1:2] = pick(done & (prev == home), owner * SLOTS + pair_rank, cache_slot)
+    tab_ref[2:3] = pack // NS * NR + pack % NS
+    tab_ref[3:4] = order
+    tab_ref[4:5] = order // SLOTS * 16 + order % SLOTS
+    tab_ref[5:6] = pick(owned, home_slot, cache_order.astype(F32))
+    tab_ref[6:7] = pick(owned, home_slot, jnp.ones((1, n), F32))
+    tab_ref[7:8] = jnp.zeros((1, width), jnp.int32)
 
 
 def shards(
@@ -412,28 +453,15 @@
     HID = lm_resid.shape[1]
     AW = lm_adapt.shape[1]
 
-    tables = routing(complete, owner, prev_owner, S, SH, home, NS, NR)
-    first = (home * U + lax.axis_index("sub")) * NS
-    lengths = lax.dynamic_slice_in_dim(lm_lengths, first, NS, 0)
+    n = owner.shape[0]
+    tables = pl.pallas_call(
+        functools.partial(routing_kernel, (S, SH, NS, NR)),
+        out_shape=jax.ShapeDtypeStruct((8, up(SL, 128)), jnp.int32),
+        compiler_params=pltpu.CompilerParams(vmem_limit_bytes=60 * 1024 * 1024),
+    )(complete.reshape(1, n), owner.reshape(1, n), prev_owner.reshape(1, n))
     LR = 2 * lm_cache.shape[1]
-    lanes = jnp.arange(LR)
-    bias = jnp.where(
-        (lanes % 2 == 0)[None, :] & (lanes[None, :] < 2 * lengths[:, None]), 0.0, NEG
-    ).astype(F32)[:, None, :]
-    q = jnp.transpose(lm_query.reshape(NS, KV, R, HEAD_WIDTH), (1, 0, 2, 3))
-    q = jnp.pad(q, ((0, 0), (0, 0), (0, 8 - R), (0, 0)))
     lmx = lm_cache.reshape(NS, LR, KV * HEAD_WIDTH)
-    pair = jnp.transpose(
-        language_new_pair.astype(F32).reshape(NS, 2, KV, HEAD_WIDTH), (1, 2, 0, 3)
-    )[:, :, :, None, :]
-    resid = jnp.pad(lm_resid.reshape(U, NS, HID), ((0, 0), (0, NR - NS), (0, 0))).reshape(M, HID)
-    state = (
-        det_noise.astype(F32) + jnp.pad(det_pending, ((0, 0), (0, 1), (0, 0))).astype(F32)
-    ).astype(BF16)
-    state = jnp.pad(state, ((0, 0), (0, TOK - span), (0, 0)))
-    dcache = jnp.pad(
-        det_cache.reshape(SH, 2 * past, CW), ((0, 0), (0, XR - 2 * past), (0, 0))
-    )
+    dcache = det_cache.reshape(SH, past, 2, CW)
     sizes = (S, T, U)
     V = pl.BlockSpec(memory_space=pltpu.VMEM)
     SM = pl.BlockSpec(memory_space=pltpu.SMEM)
@@ -442,7 +470,8 @@
     dma = pltpu.SemaphoreType.DMA
     scratch = [
         v(lm_wo.shape, BF16), v(lm_adapt.shape, BF16), v(det_qkv.shape, BF16),
-        v(det_out.shape, BF16),
+        v(det_out.shape, BF16), v((NS, 1, LR), F32), v((KV, NS, 8, HEAD_WIDTH), F32),
+        v((M, HID), F32),
         v((SL, TOK, CW), BF16), v((SL, TOK, CW), BF16),
         v((SL, XR, CW), BF16), v((SL, XR, CW), BF16),
         v((U, NR, QW), BF16), v((T, M, HID), BF16), v((U, M, AW + 128), F32),
@@ -460,21 +489,20 @@
     hidden, new_state = pl.pallas_call(
         functools.partial(kernel, sizes, past),
         out_shape=(
-            jax.ShapeDtypeStruct((M, HID), BF16),
+            jax.ShapeDtypeStruct((SH, HID), BF16),
             jax.ShapeDtypeStruct((SL, span, CW), BF16),
         ),
-        in_specs=[SM] * 7 + [V] * 10 + [ANY] * 4,
+        in_specs=[SM] * 2 + [V] * 9 + [ANY] * 4,
         out_specs=(V, V),
         scratch_shapes=scratch,
         compiler_params=pltpu.CompilerParams(
             collective_id=0, has_side_effects=True, vmem_limit_bytes=60 * 1024 * 1024
         ),
     )(
-        *tables, state, dcache, q, lmx, pair[0], pair[1], bias, resid,
-        lm_gain.astype(F32)[None, :], det_gain.astype(F32)[None, :],
+        tables, lm_lengths, det_noise, det_pending, dcache, lm_query, lmx, language_new_pair,
+        lm_resid, lm_gain[None, :], det_gain[None, :],
         lm_wo, lm_adapt, det_qkv, det_out,
     )
-    hidden = hidden.reshape(U, NR, HID)[:, :NS].reshape(SH, HID)
     return hidden, new_state.reshape(1, S, SLOTS, span, CW)
 
 

time: 105 us -> 91 us (0.87)
  the two profiles are of different devices: /device:TPU:0 before, /device:TPU:9 now
where the time goes in v1:
time: 91 us; the launch traced here: 90.7 us
  Pallas kernels  79 us (87%)
  local copies, waits for them, and re-layouts  11 us (12%)
    pallas_call x1, Pallas kernels, shards(): pl.pallas_call(functools.partial(kernel, sizes, past), out_shape=(jax.Sha...  77.4 us
    unnamed x6, local copies, waits for them, and re-layouts  7.19 us

profile of v1, /device:TPU:9, one launch (start us, length us, event | category | flops | bytes accessed | tf_op | source)
XLA Modules:
  0.0 90.7 jit_solution(2252765894405656750)
XLA Ops:
  0.6 0.0 copy-start
  0.6 1.4 %broadcast_in_dim.7.dgain_ref = bf16[1,1024]{1,0:T(2,128)(2,1)} reshape(bf16[1024]{0:T(1024)(128)(2,1)} %param.30) | data formatting | bytes 4096 | tf_op jit(solution)/shard_map/broadcast_in_dim | solution.py:503
  2.0 1.6 %shard_map.176.tab_ref = s32[8,128]{1,0:T(8,128)} custom-call(s32[1,96]{1,0:T(1,128)} %bitcast.7, s32[1,96]{1,0:T(1,128)} %bitcast.8, s32[1,96]{1,0:T(1,128)} %bitcast.9), custom_call_target="tpu_custom_call" | custom-call | tf_op jit(solution)/shard_map/pallas_call | solution.py:457
  3.6 1.3 %broadcast_in_dim.6.gain_ref = bf16[1,1792]{1,0:T(2,128)(2,1)} reshape(bf16[1792]{0:T(1024)(128)(2,1)} %param.23) | data formatting | bytes 7168 | tf_op jit(solution)/shard_map/broadcast_in_dim | solution.py:503
  4.9 1.8 %copy.19.noise_ref = bf16[24,30,256]{2,1,0:T(8,128)(2,1)} copy(bf16[24,30,256]{2,0,1:T(8,128)(2,1)} %param.25) | data formatting | bytes 737280 | tf_op args[8]
  6.7 1.8 %copy.20.pend_ref = bf16[24,29,256]{2,1,0:T(8,128)(2,1)} copy(bf16[24,29,256]{2,0,1:T(8,128)(2,1)} %param.26) | data formatting | bytes 712704 | tf_op args[9]
  8.6 0.0 copy-done
  8.6 1.2 %reshape.26.lmx_ref = bf16[12,128,256]{2,1,0:T(8,128)(2,1)} reshape(bf16[12,64,2,256]{3,2,1,0:T(2,128)(2,1)S(1)} %copy-done) | data formatting | bytes 1572864 | tf_op jit(solution)/shard_map/reshape | solution.py:463
  9.7 77.4 %shard_map.177 = (bf16[24,1792]{1,0:T(8,128)(2,1)}, bf16[24,30,256]{2,1,0:T(8,128)(2,1)}) custom-call(s32[8,128]{1,0:T(8,128)} %shard_map.176.tab_ref, s32[96]{0:T(128)} %len_ref.1, bf16[24,30,256]{2,1,0:T(8,128)(2,1)} %copy.19.noise_ref, bf16[24,29,256]{2,1,0:T(8,128)(2,1)} %copy.20.pend_ref, bf16[24,60,2,256]{3,2,1,0:T(2,128)(2,1)} %bitcast.5, ...), custom_call_target="tpu_custom_call" | custom-call | tf_op jit(solution)/shard_map/pallas_call | solution.py:489
  87.1 2.0 %copy.21 = bf16[1,4,6,30,256]{4,1,3,2,0:T(4,128)(2,1)} copy(bf16[1,4,6,30,256]{4,3,2,1,0:T(8,128)(2,1)} %bitcast.6) | data formatting | bytes 737280
  89.2 1.5 %copy.23 = bf16[24,1792]{1,0:T(8,128)(2,1)} copy(bf16[24,1792]{1,0:T(8,128)(2,1)} %get-tuple-element.10) | data formatting | bytes 172032
Async XLA Ops:
  0.6 7.9 %copy-start = (bf16[12,64,2,256]{3,2,1,0:T(2,128)(2,1)S(1)}, bf16[12,64,2,256]{3,2,1,0:T(2,128)(2,1)}, u32[]{:S(2)}) copy-start(bf16[12,64,2,256]{3,2,1,0:T(2,128)(2,1)} %param.18) | copy-start | bytes 2359300

commit v2 on v1

--- a/solution.py
+++ b/solution.py
@@ -38,9 +38,9 @@
     hid_ref, out_ref,
     wo, adapt, qkv, dout, bias_s, q_s, resid_s,
     stsend, strecv, csend, crecv, att_all, parts, condx, condf, condpack, condsend, condrecv,
-    condrf, gath, n29, lg, lgf, a_s, qb, kb, vb, mx, own, osend, orecv, res,
+    condrf, gath, n29, lg, lgf, a_s, qb, kb, vb, mx, own, ocs, ocr, oxs, oxr, res,
     w_sem, st_s, st_r, ca_s, ca_r, co_s, co_r, at_s, at_r, pa_s, pa_r, cx_s, cx_r,
-    g_s, g_r, l_s, l_r, o_s, o_r,
+    g_s, g_r, gc_s, gc_r, l_s, l_r, oc_s, oc_r, o_s, o_r,
 ):
     S, T, U = sizes
     past = 2 * past_len
@@ -55,6 +55,10 @@
     R = QUERY_HEADS // KEY_VALUE_HEADS
     last = out_ref.shape[1] - 1
 
+    def row_of(ref):
+        g = ref[...].astype(F32)
+        return jnp.concatenate([g[i:i + 1] for i in range(g.shape[0])], axis=1)
+
     def at_stream(d):
         return {"stream": lax.rem(me + d, S)}
 
@@ -108,7 +112,10 @@
         csend[i, 0:past] = row
         return 0
 
-    lax.fori_loop(0, SL, pack_cache, 0)
+    def pack_block(d):
+        o = lax.rem(me + d, S)
+        lax.fori_loop(o * SLOTS, o * SLOTS + SLOTS, pack_cache, 0)
+
     ca_copies = [None]
 
     def send_cache(d):
@@ -119,6 +126,7 @@
         )
 
     for d in range(1, S // 2):
+        pack_block(d)
         send_cache(d)
 
     def keep_own(i, _):
@@ -127,7 +135,6 @@
         crecv[c] = csend[c]
         return 0
 
-    lax.fori_loop(0, SLOTS, keep_own, 0)
 
     scale = HEAD_WIDTH ** (-0.5)
     LR = bias_s.shape[2]
@@ -152,7 +159,7 @@
     for kv in range(KV):
         q = q_s[kv]
         pair_kv = pair[:, :, kv * HEAD_WIDTH:(kv + 1) * HEAD_WIDTH]
-        x = lmx_ref[:, :, kv * HEAD_WIDTH:(kv + 1) * HEAD_WIDTH]
+        x = lmx_ref[:, :, :, kv * HEAD_WIDTH:(kv + 1) * HEAD_WIDTH].reshape(NS, LR, HEAD_WIDTH)
         s = lax.dot_general(q.astype(BF16), x, (((2,), (2,)), ((0,), (0,))), preferred_element_type=F32)
         s = s * scale + bias
         s_new = jnp.sum(q * pair_kv[:, 0:1], axis=-1, keepdims=True) * scale
@@ -174,6 +181,11 @@
             send(att_all.at[u_me], att_all.at[u_me], at_s.at[d], at_r.at[d],
                  {"sub": lax.rem(u_me + d, U)})
         )
+    late = list(range(max(1, S // 2), S))
+    pack_block(0)
+    lax.fori_loop(0, SLOTS, keep_own, 0)
+    for d in late[:len(late) // 2]:
+        pack_block(d)
     for c in at_copies:
         c.wait_recv()
     loads[0].wait()
@@ -186,6 +198,8 @@
             send(parts.at[t_me], parts.at[t_me], pa_s.at[d], pa_r.at[d],
                  {"tensor": lax.rem(t_me + d, T)})
         )
+    for d in late[len(late) // 2:]:
+        pack_block(d)
     for c in st_copies:
         c.wait_recv()
 
@@ -198,9 +212,22 @@
     lax.fori_loop(0, SL, arrange, 0)
     for c in pa_copies:
         c.wait_recv()
-    g_copies = []
-    for d in range(1, NP):
-        g_copies.append(send(gath.at[p_me], gath.at[p_me], g_s.at[d], g_r.at[d], at_part(d)))
+    g_copies, gc_copies = [], []
+
+    def share(j, part):
+        for e in range(1, U):
+            i = (e - 1) * T + j
+            gc_copies.append(
+                send(gath.at[part], gath.at[part], gc_s.at[i], gc_r.at[i],
+                     {"sub": lax.rem(u_me + e, U)})
+            )
+
+    for d in range(1, T):
+        g_copies.append(
+            send(gath.at[p_me], gath.at[p_me], g_s.at[d], g_r.at[d],
+                 {"tensor": lax.rem(t_me + d, T)})
+        )
+    share(0, p_me)
     mixing = parts[0].astype(F32)
     for t in range(1, T):
         mixing = mixing + parts[t].astype(F32)
@@ -208,7 +235,7 @@
     for u in range(U):
         hid_ref[u * NS:(u + 1) * NS] = hidden[u * NR:u * NR + NS]
     wide = hidden.astype(F32)
-    gained = (wide * gain_ref[...].astype(F32)).astype(BF16)
+    gained = (wide * row_of(gain_ref)).astype(BF16)
     loads[1].wait()
     AW = adapt.shape[1]
     condx[u_me, :, 0:AW] = jnp.dot(gained, adapt[...], preferred_element_type=F32)
@@ -245,10 +272,13 @@
         co_copies.append(
             send(condsend.at[o], condrecv.at[me], co_s.at[d], co_r.at[d], at_stream(d))
         )
-    for d in range(max(1, S // 2), S):
+    for d in late:
         send_cache(d)
     condrecv[me] = condsend[me]
     lgf[...] = jnp.zeros(lgf.shape, F32)
+    for d in range(1, T):
+        g_copies[d - 1].wait_recv()
+        share(d, lax.rem(t_me - d + T, T) * U + u_me)
     for c in co_copies:
         c.wait_recv()
     condrf[...] = condrecv[...].astype(F32).reshape(condrf.shape)
@@ -262,7 +292,7 @@
     l_copies = []
     for d in range(1, NP):
         l_copies.append(send(lg.at[p_me], lg.at[p_me], l_s.at[d], l_r.at[d], at_part(d)))
-    for c in g_copies:
+    for c in gc_copies:
         c.wait_recv()
     for c in l_copies:
         c.wait_recv()
@@ -273,7 +303,7 @@
     def full_rows(part, c):
         return jnp.where(is_last, lgf[part, pl.ds(c, 1), :], gath[part, c].astype(F32))
 
-    dgain = dgain_ref[...].astype(F32)
+    dgain = row_of(dgain_ref)
 
     def normalize(c, _):
         rows = [full_rows(pt, c) for pt in range(NP)]
@@ -312,7 +342,25 @@
     bias_c = jnp.where((key_lane % 2 == 0) & (key_lane < past), 0.0, NEG)
     bias_o = jnp.where(lax.broadcasted_iota(jnp.int32, (1, TOK), 1) <= last, 0.0, NEG)
 
-    o_copies = []
+    o_copies = [[] for _ in range(S)]
+    oc_copies = [[] for _ in range(S)]
+
+    def across(d):
+        for c in oc_copies[d]:
+            c.wait_recv()
+        for j in list(range(1, T)) + [0]:
+            y = own[d, j]
+            for e in range(1, U):
+                y = y + ocr[e - 1, d, j].astype(F32)
+            if j == 0:
+                own[d, j] = y
+            else:
+                oxs[j - 1, d] = y.astype(BF16)
+                o_copies[d].append(
+                    send(oxs.at[j - 1, d], oxr.at[j - 1, d], o_s.at[j, d], o_r.at[j, d],
+                         {"tensor": lax.rem(t_me + j, T)})
+                )
+
     for d in range(S):
         p = lax.rem(me - d + S, S)
         if d > 0:
@@ -341,27 +389,31 @@
             return 0
 
         lax.fori_loop(0, SLOTS, attend, 0, unroll=True)
-        for e in range(NP):
-            pt = lax.rem(p_me + e, NP)
-            y = jnp.dot(
-                mx[...], dout[:, pl.ds(pl.multiple_of(pt * CW, 128), CW)],
-                preferred_element_type=F32,
-            )
-            if e == 0:
-                own[d] = y
-            else:
-                osend[e, d] = y.astype(BF16)
-                o_copies.append(
-                    send(osend.at[e, d], orecv.at[e, d], o_s.at[e, d], o_r.at[e, d], at_part(e))
+        for e in range(U):
+            u = lax.rem(u_me + e, U)
+            for j in range(T):
+                pt = lax.rem(t_me + j, T) * U + u
+                y = jnp.dot(
+                    mx[...], dout[:, pl.ds(pl.multiple_of(pt * CW, 128), CW)],
+                    preferred_element_type=F32,
                 )
-    i = 0
+                if e == 0:
+                    own[d, j] = y
+                else:
+                    ocs[e - 1, d, j] = y.astype(BF16)
+            if e > 0:
+                oc_copies[d].append(
+                    send(ocs.at[e - 1, d], ocr.at[e - 1, d], oc_s.at[e, d], oc_r.at[e, d], {"sub": u})
+                )
+        if d > 0:
+            across(d - 1)
+    across(S - 1)
     for d in range(S):
         p = lax.rem(me - d + S, S)
-        mix = own[d]
-        for e in range(1, NP):
-            o_copies[i].wait_recv()
-            mix = mix + orecv[e, d].astype(F32)
-            i += 1
+        mix = own[d, 0]
+        for j in range(1, T):
+            o_copies[d][j - 1].wait_recv()
+            mix = mix + oxr[j - 1, d].astype(F32)
         mix = mix.reshape(SLOTS, TOK, CW)
         for k in range(SLOTS):
             c = p * SLOTS + k
@@ -374,8 +426,8 @@
         return 0
 
     lax.fori_loop(0, SL, write, 0)
-    for c in (st_copies + ca_copies[1:] + at_copies + pa_copies + g_copies + cx_copies
-              + co_copies + l_copies + o_copies):
+    for c in (sum(o_copies, []) + sum(oc_copies, []) + gc_copies + st_copies + ca_copies[1:] + at_copies + pa_copies + g_copies + cx_copies
+              + co_copies + l_copies):
         c.wait_send()
 
 
@@ -460,7 +512,6 @@
         compiler_params=pltpu.CompilerParams(vmem_limit_bytes=60 * 1024 * 1024),
     )(complete.reshape(1, n), owner.reshape(1, n), prev_owner.reshape(1, n))
     LR = 2 * lm_cache.shape[1]
-    lmx = lm_cache.reshape(NS, LR, KV * HEAD_WIDTH)
     dcache = det_cache.reshape(SH, past, 2, CW)
     sizes = (S, T, U)
     V = pl.BlockSpec(memory_space=pltpu.VMEM)
@@ -479,12 +530,14 @@
         v((S * 16, CW), F32), v((NP, SL, TOK, CW), BF16), v((CL, CW), F32),
         v((NP, CL, CW), BF16), v((NP, CL, CW), F32), v((SL, TOK, NP * CW), BF16),
         v((SL, TOK, CW), BF16), v((SL, TOK, CW), BF16), v((SL, TOK, CW), BF16),
-        v((SLOTS * TOK, CW), BF16), v((S, SLOTS * TOK, CW), F32),
-        v((NP, S, SLOTS * TOK, CW), BF16), v((NP, S, SLOTS * TOK, CW), BF16),
+        v((SLOTS * TOK, CW), BF16), v((S, T, SLOTS * TOK, CW), F32),
+        v((U - 1, S, T, SLOTS * TOK, CW), BF16), v((U - 1, S, T, SLOTS * TOK, CW), BF16),
+        v((T - 1, S, SLOTS * TOK, CW), BF16), v((T - 1, S, SLOTS * TOK, CW), BF16),
         v((SL, TOK, CW), F32),
         dma((4,)), dma((S,)), dma((S,)), dma((S,)), dma((S,)), dma((S,)), dma((S,)),
         dma((U,)), dma((U,)), dma((T,)), dma((T,)), dma((U,)), dma((U,)),
-        dma((NP,)), dma((NP,)), dma((NP,)), dma((NP,)), dma((NP, S)), dma((NP, S)),
+        dma((T,)), dma((T,)), dma((U * T,)), dma((U * T,)), dma((NP,)), dma((NP,)),
+        dma((U, S)), dma((U, S)), dma((T, S)), dma((T, S)),
     ]
     hidden, new_state = pl.pallas_call(
         functools.partial(kernel, sizes, past),
@@ -499,8 +552,8 @@
             collective_id=0, has_side_effects=True, vmem_limit_bytes=60 * 1024 * 1024
         ),
     )(
-        tables, lm_lengths, det_noise, det_pending, dcache, lm_query, lmx, language_new_pair,
-        lm_resid, lm_gain[None, :], det_gain[None, :],
+        tables, lm_lengths, det_noise, det_pending, dcache, lm_query, lm_cache, language_new_pair,
+        lm_resid, lm_gain.reshape(-1, 128), det_gain.reshape(-1, 128),
         lm_wo, lm_adapt, det_qkv, det_out,
     )
     return hidden, new_state.reshape(1, S, SLOTS, span, CW)

time: 91 us -> 75.5 us (0.83)
  the two profiles are of different devices: /device:TPU:9 before, /device:TPU:0 now
where the time goes in v2:
time: 75.5 us; the launch traced here: 75.2 us
  Pallas kernels  67.4 us (89%)
  local copies, waits for them, and re-layouts  7.17 us (9%)
    pallas_call x1, Pallas kernels, shards(): pl.pallas_call(functools.partial(kernel, sizes, past), out_shape=(jax.Sha...  65.7 us
    unnamed x4, local copies, waits for them, and re-layouts  7.17 us
    pallas_call x1, Pallas kernels, shards(): pl.pallas_call(functools.partial(routing_kernel, (S, SH, NS, NR)), out_sh...  1.65 us

profile of v2, /device:TPU:0, one launch (start us, length us, event | category | flops | bytes accessed | tf_op | source)
XLA Modules:
  0.0 75.2 jit_solution(18060712150321957454)
XLA Ops:
  0.6 1.6 %shard_map.176.tab_ref = s32[8,128]{1,0:T(8,128)} custom-call(s32[1,96]{1,0:T(1,128)} %bitcast.11, s32[1,96]{1,0:T(1,128)} %bitcast.12, s32[1,96]{1,0:T(1,128)} %bitcast.13), custom_call_target="tpu_custom_call" | custom-call | tf_op jit(solution)/shard_map/pallas_call | solution.py:509
  2.3 1.8 %copy.19.noise_ref = bf16[24,30,256]{2,1,0:T(8,128)(2,1)} copy(bf16[24,30,256]{2,0,1:T(8,128)(2,1)} %param.25) | data formatting | bytes 737280 | tf_op args[8]
  4.1 1.8 %copy.20.pend_ref = bf16[24,29,256]{2,1,0:T(8,128)(2,1)} copy(bf16[24,29,256]{2,0,1:T(8,128)(2,1)} %param.26) | data formatting | bytes 712704 | tf_op args[9]
  5.9 65.7 %shard_map.177 = (bf16[24,1792]{1,0:T(8,128)(2,1)}, bf16[24,30,256]{2,1,0:T(8,128)(2,1)}) custom-call(s32[8,128]{1,0:T(8,128)} %shard_map.176.tab_ref, s32[96]{0:T(128)} %len_ref.1, bf16[24,30,256]{2,1,0:T(8,128)(2,1)} %copy.19.noise_ref, bf16[24,29,256]{2,1,0:T(8,128)(2,1)} %copy.20.pend_ref, bf16[24,60,2,256]{3,2,1,0:T(2,128)(2,1)} %bitcast.7, ...), custom_call_target="tpu_custom_call" | custom-call | tf_op jit(solution)/shard_map/pallas_call | solution.py:542
  71.7 2.0 %copy.21 = bf16[1,4,6,30,256]{4,1,3,2,0:T(4,128)(2,1)} copy(bf16[1,4,6,30,256]{4,3,2,1,0:T(8,128)(2,1)} %bitcast.8) | data formatting | bytes 737280
  73.7 1.5 %copy.23 = bf16[24,1792]{1,0:T(8,128)(2,1)} copy(bf16[24,1792]{1,0:T(8,128)(2,1)} %get-tuple-element.10) | data formatting | bytes 172032

commit v3 on v2

--- a/solution.py
+++ b/solution.py
@@ -116,16 +116,17 @@
         o = lax.rem(me + d, S)
         lax.fori_loop(o * SLOTS, o * SLOTS + SLOTS, pack_cache, 0)
 
-    ca_copies = [None]
+    near = sorted(range(1, S), key=lambda d: (min(d, S - d), d))
+    ca_copies = {}
 
     def send_cache(d):
         o = lax.rem(me + d, S)
-        ca_copies.append(
-            send(csend.at[pl.ds(o * SLOTS, SLOTS)], crecv.at[pl.ds(me * SLOTS, SLOTS)],
-                 ca_s.at[d], ca_r.at[d], at_stream(d))
-        )
-
-    for d in range(1, S // 2):
+        ca_copies[d] = send(
+            csend.at[pl.ds(o * SLOTS, SLOTS)], crecv.at[pl.ds(me * SLOTS, SLOTS)],
+            ca_s.at[d], ca_r.at[d], at_stream(d),
+        )
+
+    for d in near[:S // 2]:
         pack_block(d)
         send_cache(d)
 
@@ -181,7 +182,7 @@
             send(att_all.at[u_me], att_all.at[u_me], at_s.at[d], at_r.at[d],
                  {"sub": lax.rem(u_me + d, U)})
         )
-    late = list(range(max(1, S // 2), S))
+    late = near[S // 2:]
     pack_block(0)
     lax.fori_loop(0, SLOTS, keep_own, 0)
     for d in late[:len(late) // 2]:
@@ -361,10 +362,10 @@
                          {"tensor": lax.rem(t_me + j, T)})
                 )
 
-    for d in range(S):
-        p = lax.rem(me - d + S, S)
+    for d, shift in enumerate([0] + near):
+        p = lax.rem(me - shift + S, S)
         if d > 0:
-            ca_copies[d].wait_recv()
+            ca_copies[shift].wait_recv()
 
         def attend(k, _):
             c = p * SLOTS + k
@@ -408,8 +409,8 @@
         if d > 0:
             across(d - 1)
     across(S - 1)
-    for d in range(S):
-        p = lax.rem(me - d + S, S)
+    for d, shift in enumerate([0] + near):
+        p = lax.rem(me - shift + S, S)
         mix = own[d, 0]
         for j in range(1, T):
             o_copies[d][j - 1].wait_recv()
@@ -426,7 +427,7 @@
         return 0
 
     lax.fori_loop(0, SL, write, 0)
-    for c in (sum(o_copies, []) + sum(oc_copies, []) + gc_copies + st_copies + ca_copies[1:] + at_copies + pa_copies + g_copies + cx_copies
+    for c in (sum(o_copies, []) + sum(oc_copies, []) + gc_copies + st_copies + list(ca_copies.values()) + at_copies + pa_copies + g_copies + cx_copies
               + co_copies + l_copies):
         c.wait_send()
 

time: 75.5 us -> 76.2 us (level)
  no operation moved by 1% of the time
where the time goes in v3:
time: 76.2 us; the launch traced here: 75.9 us
  Pallas kernels  68.1 us (89%)
  local copies, waits for them, and re-layouts  7.17 us (9%)
    pallas_call x1, Pallas kernels, shards(): pl.pallas_call(functools.partial(kernel, sizes, past), out_shape=(jax.Sha...  66.5 us
    unnamed x4, local copies, waits for them, and re-layouts  7.17 us
    pallas_call x1, Pallas kernels, shards(): pl.pallas_call(functools.partial(routing_kernel, (S, SH, NS, NR)), out_sh...  1.65 us

profile of v3, /device:TPU:0, one launch (start us, length us, event | category | flops | bytes accessed | tf_op | source)
XLA Modules:
  0.0 75.9 jit_solution(11698554150248031681)
XLA Ops:
  0.6 1.6 %shard_map.176.tab_ref = s32[8,128]{1,0:T(8,128)} custom-call(s32[1,96]{1,0:T(1,128)} %bitcast.11, s32[1,96]{1,0:T(1,128)} %bitcast.12, s32[1,96]{1,0:T(1,128)} %bitcast.13), custom_call_target="tpu_custom_call" | custom-call | tf_op jit(solution)/shard_map/pallas_call | solution.py:510
  2.3 1.8 %copy.19.noise_ref = bf16[24,30,256]{2,1,0:T(8,128)(2,1)} copy(bf16[24,30,256]{2,0,1:T(8,128)(2,1)} %param.25) | data formatting | bytes 737280 | tf_op args[8]
  4.1 1.8 %copy.20.pend_ref = bf16[24,29,256]{2,1,0:T(8,128)(2,1)} copy(bf16[24,29,256]{2,0,1:T(8,128)(2,1)} %param.26) | data formatting | bytes 712704 | tf_op args[9]
  5.9 66.5 %shard_map.177 = (bf16[24,1792]{1,0:T(8,128)(2,1)}, bf16[24,30,256]{2,1,0:T(8,128)(2,1)}) custom-call(s32[8,128]{1,0:T(8,128)} %shard_map.176.tab_ref, s32[96]{0:T(128)} %len_ref.1, bf16[24,30,256]{2,1,0:T(8,128)(2,1)} %copy.19.noise_ref, bf16[24,29,256]{2,1,0:T(8,128)(2,1)} %copy.20.pend_ref, bf16[24,60,2,256]{3,2,1,0:T(2,128)(2,1)} %bitcast.7, ...), custom_call_target="tpu_custom_call" | custom-call | tf_op jit(solution)/shard_map/pallas_call | solution.py:543
  72.4 2.0 %copy.21 = bf16[1,4,6,30,256]{4,1,3,2,0:T(4,128)(2,1)} copy(bf16[1,4,6,30,256]{4,3,2,1,0:T(8,128)(2,1)} %bitcast.8) | data formatting | bytes 737280
  74.4 1.5 %copy.23 = bf16[24,1792]{1,0:T(8,128)(2,1)} copy(bf16[24,1792]{1,0:T(8,128)(2,1)} %get-tuple-element.10) | data formatting | bytes 172032
